TPU v7x, 32 devices: a whole 2x2x4 slice. The times are simulated.
32 devices in a mesh: grid: 2 (over x), rank: 4 (over y, core), term: 4 (over z).
Axes of the slice: x: 2, y: 2, z: 4, core: 2. Of those that a mesh axis runs over, the one named last changes fastest.
Arguments:
- rhs: float32 [128, 4, 256], P('rank', 'grid')
- coef: float32 [12, 4, 256], P('term', 'grid'), may hold values from 0.03 to 0.3
- env: float32 [12, 128, 128], P('term', 'rank'), as said below
Outputs:
- solution: float32 [128, 4, 256], P('rank', 'grid')
- residual: float32 [128, 4, 256], P('rank', 'grid')
Inputs may be any that keep to these rules, and one draw needn't show every extreme that they name: env[k] is a symmetric matrix for every k.
All inputs are finite; a program needn't handle non-finite values.
Results may differ from a plain program's by a relative error of at most 0.0003.
Values sent between devices are 32-bit elements; how exact they have to be, the bound alone decides.
A program may use at most 64 MiB of HBM per device.

v0:
```python
import functools

import jax
import jax.numpy as jnp
from jax import lax
from jax.experimental import pallas as pl
from jax.experimental.pallas import tpu as pltpu
from jax.sharding import PartitionSpec as P

ITERS = 4
MESH = pl.DeviceIdType.MESH


def padded_2(block, sides, width):
    for axis, dim in sides:
        count = lax.axis_size(axis)
        forward = [(i, i + 1) for i in range(count - 1)]
        backward = [(target, source) for source, target in forward]
        low = lax.ppermute(
            lax.slice_in_dim(block, block.shape[dim] - width, None, axis=dim), axis, forward
        )
        high = lax.ppermute(lax.slice_in_dim(block, 0, width, axis=dim), axis, backward)
        block = jnp.concatenate([low, block, high], axis=dim)
    return block


def face_weights(padded):
    wide = jnp.pad(padded, ((0, 0), (0, 0), (1, 1)))
    centre = wide[:, 1:-1, 1:-1]
    face_up = 0.5 * (centre + wide[:, 2:, 1:-1])
    face_down = 0.5 * (centre + wide[:, :-2, 1:-1])
    face_right = 0.5 * (centre + wide[:, 1:-1, 2:])
    face_left = 0.5 * (centre + wide[:, 1:-1, :-2])
    return (face_up + face_down + face_right + face_left, face_up, face_down, face_right, face_left)


def apply_faces(field, faces):
    middle = field[..., 1:-1, :]
    sideways = jnp.pad(middle, [(0, 0)] * (middle.ndim - 1) + [(1, 1)])
    total, face_up, face_down, face_right, face_left = faces
    return (
        total * middle
        - face_up * field[..., 2:, :]
        - face_down * field[..., :-2, :]
        - face_right * sideways[..., 2:]
        - face_left * sideways[..., :-2]
    )


def shards(rhs, coef, env):
    coef_padded = padded_2(coef, (("grid", 1),), 1)
    faces = tuple((weights[:, None] for weights in face_weights(coef_padded)))

    def square_sum(vector):
        return lax.psum(jnp.sum(vector * vector), ("grid", "rank"))

    solution = jnp.zeros(rhs.shape, jnp.float32)
    residual = rhs
    direction = rhs
    norm_now = square_sum(residual)
    for step in range(ITERS):
        padded = padded_2(direction, (("grid", 1),), 1)
        stenciled = apply_faces(padded[None], faces)
        image = lax.psum_scatter(
            jnp.einsum("krs,krxy->sxy", env, stenciled, precision=lax.Precision.HIGHEST),
            "rank",
            scatter_dimension=0,
            tiled=True,
        )
        image = lax.psum(image, "term")
        alpha = norm_now / lax.psum(jnp.sum(direction * image), ("grid", "rank"))
        solution = solution + alpha * direction
        residual = residual - alpha * image
        norm_next = square_sum(residual)
        direction = residual + norm_next / norm_now * direction
        norm_now = norm_next
    return (solution, residual)


def shift_sum(v):
    lane = lax.broadcasted_iota(jnp.int32, v.shape, v.ndim - 1)
    n = v.shape[-1]
    axis = v.ndim - 1
    left = jnp.where(lane == 0, 0.0, pltpu.roll(v, 1, axis))
    right = jnp.where(lane == n - 1, 0.0, pltpu.roll(v, n - 1, axis))
    return left + right


def neighbours(read, x, count):
    total = shift_sum(read(x))
    if x > 0:
        total = total + read(x - 1)
    if x < count - 1:
        total = total + read(x + 1)
    return total


def split3(v):
    high = v.astype(jnp.bfloat16)
    low = (v - high.astype(jnp.float32)).astype(jnp.bfloat16)
    return jnp.concatenate([high, high, low], axis=0)


def total_sum(v):
    return jnp.sum(v, axis=(0, 1), keepdims=True)


def cg_kernel(
    sizes,
    rhs_ref, coef_ref, env_ref,
    sol_ref, out_ref,
    rhs_own, env_all, coef_all, coef_tab, diag_tab, stack, residual, direction, image, partial, weighted, dots,
    load, rhs_send, rhs_recv, sib_send, sib_recv, env_send, env_recv, envy_send, envy_recv,
    coef_send, coef_recv, img_send, img_recv, dot_send, dot_recv,
):
    terms, per, rows, strip, ny, ranks = sizes
    grids, ys = 2, 2
    nx = grids * strip
    half = ys * rows
    gx = lax.axis_index("grid")
    rank = lax.axis_index("rank")
    gz = lax.axis_index("term")
    gy = rank // 2
    core = rank % 2
    sibling = (gx, gy * 2 + (1 - core), gz)

    def at(x, y, z):
        return (x, y * 2 + core, z)

    origins = [gz + 1 - 2 * (gz % 2), 2 - gz // 2, 3 - 3 * (gz // 2)]
    over_x, over_y, across = at(1 - gx, gy, gz), at(gx, 1 - gy, gz), at(1 - gx, 1 - gy, gz)
    line = [at(gx, gy, o) for o in origins]

    loads = [
        pltpu.make_async_copy(rhs_ref, rhs_own, load.at[0]),
        pltpu.make_async_copy(env_ref, env_all.at[gz, :, gy], load.at[1]),
        pltpu.make_async_copy(coef_ref, coef_all.at[gz, gx], load.at[2]),
    ]
    for copy in loads:
        copy.start()

    barrier = pltpu.get_barrier_semaphore()

    def greet(peer):
        pl.semaphore_signal(barrier, inc=1, device_id=peer, device_id_type=MESH)

    peers = line + [over_x, over_y, across, sibling]
    for peer in peers:
        greet(peer)

    loads[0].wait()
    for i in range(strip):
        residual[gx * strip + i, gy, core] = rhs_own[:, i, :]
    loads[1].wait()
    loads[2].wait()
    pl.semaphore_wait(barrier, len(peers))

    sent = []

    def remote(src, dst, send, recv, device):
        return pltpu.make_async_remote_copy(
            src_ref=src, dst_ref=dst, send_sem=send, recv_sem=recv, device_id=device, device_id_type=MESH
        )

    def push(block, send, recv, device):
        copy = remote(block, block, send, recv, device)
        sent.append(copy)
        copy.start()
        return copy

    def arrived(block, recv):
        remote(block, block, dot_send, recv, sibling).wait_recv()

    def strip_of(x, y):
        return residual.at[pl.ds(x * strip, strip), y, core]

    def env_line(o):
        return env_all.at[o, :, gy]

    own = strip_of(gx, gy)
    for i in (2, 1, 0):
        push(env_line(gz), env_send.at[i], env_recv.at[gz], line[i])
    rhs_y = push(own, rhs_send.at[0], rhs_recv.at[0], over_y)
    rhs_x = push(own, rhs_send.at[1], rhs_recv.at[1], over_x)
    rhs_d = push(own, rhs_send.at[2], rhs_recv.at[2], across)
    for i in (2, 1, 0):
        push(coef_all.at[gz, gx], coef_send.at[i], coef_recv.at[gz], line[i])
    push(env_line(gz), envy_send.at[3], envy_recv.at[gz], over_y)
    sibs = [push(own, sib_send.at[0], sib_recv.at[0], sibling)]

    def put_stack(o):
        for i in range(per):
            block = env_all[o, i].reshape(half, ranks)
            high = block.astype(jnp.bfloat16)
            low = (block - high.astype(jnp.float32)).astype(jnp.bfloat16)
            at = pl.ds(pl.multiple_of((o * per + i) * half, half), half)
            stack[at, 0:ranks] = high
            stack[at, ranks : 2 * ranks] = low
            stack[at, 2 * ranks : 3 * ranks] = high

    def cross(i):
        o = origins[i]
        arrived(env_line(o), env_recv.at[o])
        push(env_line(o), envy_send.at[i], envy_recv.at[o], over_y)

    def to_sibling(i, copy, x, y):
        copy.wait_recv()
        sibs.append(push(strip_of(x, y), sib_send.at[i], sib_recv.at[i], sibling))

    def crossed_into_stack(o):
        arrived(env_all.at[o, :, 1 - gy], envy_recv.at[o])
        put_stack(o)

    cross(0)
    to_sibling(1, rhs_y, gx, 1 - gy)
    to_sibling(2, rhs_x, 1 - gx, gy)
    to_sibling(3, rhs_d, 1 - gx, 1 - gy)
    cross(1)
    for o in origins:
        arrived(coef_all.at[o, gx], coef_recv.at[o])
    coef_x = push(coef_all.at[:, gx], coef_send.at[terms - 1], coef_recv.at[gz], over_x)
    cross(2)
    coef_x.wait_recv()
    for x in range(nx):
        for z in range(terms):
            for i in range(per):
                k = z * per + i
                coef_tab[x, k : k + 1, :] = coef_all[z, x // strip, i, x % strip : x % strip + 1, :]
    for x in range(nx):
        diag_tab[x] = 0.5 * neighbours(lambda j: coef_tab[j], x, nx)
    for copy in sibs:
        copy.wait_recv()
    square = jnp.zeros((ranks, ny), jnp.float32)
    for x in range(nx):
        field = residual[x].reshape(ranks, ny)
        direction[x] = field
        square = square + field * field
    norm_now = total_sum(square)
    for o in [gz] + origins:
        crossed_into_stack(o)
    for copy in sent:
        copy.wait_send()

    count = terms * per

    def product(x):
        field = direction[x]
        wide = 2.0 * field - 0.5 * neighbours(lambda j: direction[j], x, nx)
        plain = jnp.dot(stack[...], split3(field), preferred_element_type=jnp.float32)
        spread = jnp.dot(stack[...], split3(wide), preferred_element_type=jnp.float32)
        total = jnp.zeros((half, ny), jnp.float32)
        inner = jnp.zeros((half, ny), jnp.float32)
        for k in range(count):
            c = coef_tab[x, k : k + 1, :]
            d = diag_tab[x, k : k + 1, :]
            u = plain[k * half : (k + 1) * half]
            total = total + c * spread[k * half : (k + 1) * half] + d * u
            inner = inner + c * u
        partial[x] = total
        weighted[x] = inner

    def finish(x, slot):
        value = partial[x] - 0.5 * neighbours(lambda j: weighted[j], x, nx)
        image[slot, x, :, core] = value.reshape(ys, rows, ny)

    def image_copy(x, slot):
        block = image.at[slot, x, :, core]
        return remote(block, block, img_send.at[slot, x], img_recv.at[slot, x], sibling)

    def operate(slot, send):
        for x in range(nx + 1):
            if x < nx:
                product(x)
            if x > 0:
                finish(x - 1, slot)
                if send:
                    image_copy(x - 1, slot).start()

    strips = pl.ds(gx * strip, strip)

    def iteration(step, norm_now):
        slot = step % 2
        operate(slot, True)
        product_sum = jnp.zeros((ranks, ny), jnp.float32)
        for x in range(nx):
            image_copy(x, slot).wait_recv()
            product_sum = product_sum + direction[x] * image[slot, x].reshape(ranks, ny)
        alpha = norm_now / total_sum(product_sum)
        square = jnp.zeros((ranks, ny), jnp.float32)
        for x in range(nx):
            fresh = residual[x].reshape(ranks, ny) - alpha * image[slot, x].reshape(ranks, ny)
            residual[x] = fresh.reshape(ys, 2, rows, ny)
            square = square + fresh * fresh
        norm_next = total_sum(square)
        beta = norm_next / norm_now
        mine = pl.ds(pl.multiple_of(rank * rows, rows), rows)
        for i in range(strip):
            sol_ref[i] = sol_ref[i] + alpha * direction[gx * strip + i, mine, :]
        for x in range(nx):
            direction[x] = residual[x].reshape(ranks, ny) + beta * direction[x]
        for x in range(nx):
            image_copy(x, slot).wait_send()
        return norm_next

    sol_ref[...] = jnp.zeros_like(sol_ref)
    norm_now = lax.fori_loop(0, ITERS - 1, iteration, norm_now)

    slot = (ITERS - 1) % 2
    operate(slot, False)
    mine = pl.ds(pl.multiple_of(rank * rows, rows), rows)
    part = jnp.zeros((rows, ny), jnp.float32)
    for x in range(nx):
        for y in range(ys):
            field = direction[x, pl.ds(pl.multiple_of((y * 2 + core) * rows, rows), rows), :]
            part = part + field * image[slot, x, y, core]
    dots[core] = jnp.broadcast_to(total_sum(part), (8, 128))
    copy = remote(dots.at[core], dots.at[core], dot_send, dot_recv, sibling)
    copy.start()
    copy.wait()
    both = dots[0] + dots[1]
    alpha = norm_now / both[0:1, 0:1]
    for i in range(strip):
        x = gx * strip + i
        sol_ref[i] = sol_ref[i] + alpha * direction[x, mine, :]
        out_ref[i] = residual[x, gy, core] - alpha * image[slot, x, gy, core]


def fused(mesh, rhs, coef, env):
    terms = mesh.shape["term"]
    rows, strip, ny = rhs.shape
    per, ranks = env.shape[0], env.shape[2]
    grids, ys = 2, 2
    nx, half, count = grids * strip, ys * rows, per * terms
    sizes = (terms, per, rows, strip, ny, ranks)
    f32 = jnp.float32
    dma = pltpu.SemaphoreType.DMA
    block = jax.ShapeDtypeStruct((strip, rows, ny), f32)
    sol, res = pl.pallas_call(
        functools.partial(cg_kernel, sizes),
        out_shape=(block, block),
        in_specs=[pl.BlockSpec(memory_space=pltpu.HBM)] * 3,
        out_specs=(pl.BlockSpec(memory_space=pltpu.VMEM),) * 2,
        scratch_shapes=[
            pltpu.VMEM((rows, strip, ny), f32),
            pltpu.VMEM((terms, per, ys, rows, ranks), f32),
            pltpu.VMEM((terms, grids, per, strip, ny), f32),
            pltpu.VMEM((nx, count, ny), f32),
            pltpu.VMEM((nx, count, ny), f32),
            pltpu.VMEM((count * half, 3 * ranks), jnp.bfloat16),
            pltpu.VMEM((nx, ys, 2, rows, ny), f32),
            pltpu.VMEM((nx, ranks, ny), f32),
            pltpu.VMEM((2, nx, ys, 2, rows, ny), f32),
            pltpu.VMEM((nx, half, ny), f32),
            pltpu.VMEM((nx, half, ny), f32),
            pltpu.VMEM((2, 8, 128), f32),
            dma((3,)),
            dma((3,)), dma((3,)),
            dma((4,)), dma((4,)),
            dma((terms - 1,)), dma((terms,)),
            dma((terms,)), dma((terms,)),
            dma((terms,)), dma((terms,)),
            dma((2, nx)), dma((2, nx)),
            dma, dma,
        ],
        compiler_params=pltpu.CompilerParams(
            collective_id=0, has_side_effects=True, vmem_limit_bytes=63 * 2**20
        ),
    )(rhs, coef, env)
    return sol.transpose(1, 0, 2), res.transpose(1, 0, 2)


def fits(mesh, rhs):
    cells = rhs.shape[1] * mesh.shape["grid"] * rhs.shape[2]
    return mesh.shape["rank"] == 4 and mesh.shape["grid"] == 2 and mesh.shape["term"] == 4 and rhs.shape[0] * 4 * cells * 4 <= 2**20


def solution(mesh):
    placed = (P("rank", "grid", None), P("term", "grid", None), P("term", "rank", None))

    def run(rhs, coef, env):
        if fits(mesh, rhs):
            return fused(mesh, rhs, coef, env)
        return shards(rhs, coef, env)

    return jax.shard_map(
        run,
        mesh=mesh,
        in_specs=placed,
        out_specs=(P("rank", "grid", None), P("rank", "grid", None)),
        check_vma=False,
    )
```

profile of v0, /device:TPU:0, one launch (start us, length us, event | category | flops | bytes accessed | tf_op | source)
XLA Modules:
  0.0 33.7 jit_solution(14895144900021486737)
XLA Ops:
  0.6 30.9 %shard_map.50 = (f32[2,32,256]{2,1,0:T(8,128)}, f32[2,32,256]{2,1,0:T(8,128)}) custom-call(f32[32,2,256]{2,1,0:T(2,128)} %rhs_ref.1, f32[3,2,256]{2,1,0:T(2,128)} %coef_ref.1, f32[3,32,128]{2,1,0:T(8,128)} %env_ref.1), custom_call_target="tpu_custom_call" | custom-call | tf_op jit(solution)/shard_map/pallas_call | solution.py:338
  31.5 0.0 copy-start
  31.5 1.6 %copy.5 = f32[32,2,256]{2,1,0:T(2,128)} copy(f32[32,2,256]{2,0,1:T(8,128)} %bitcast.3) | data formatting | bytes 131072
  33.1 0.0 copy-done
  33.1 0.7 %copy.6 = f32[32,2,256]{2,1,0:T(2,128)} copy(f32[32,2,256]{2,0,1:T(8,128)S(1)} %bitcast.2) | data formatting | bytes 131072
Async XLA Ops:
  31.5 1.6 %copy-start = (f32[2,32,256]{2,1,0:T(8,128)S(1)}, f32[2,32,256]{2,1,0:T(8,128)}, u32[]{:S(2)}) copy-start(f32[2,32,256]{2,1,0:T(8,128)} %get-tuple-element.5) | copy-start | bytes 196612
where the time goes:
time: 34 us; the launch traced here: 33.7 us
  Pallas kernels  30.9 us (91%)
  local copies, waits for them, and re-layouts  2.24 us (7%)
  between operations  0.65 us (2%)
    pallas_call x1, Pallas kernels, fused(): pl.pallas_call(functools.partial(cg_kernel, sizes), out_shape=(block, blo...  30.9 us
    unnamed x4, local copies, waits for them, and re-layouts  2.24 us

commit v1 on v0

--- a/solution.py
+++ b/solution.py
@@ -9,6 +9,7 @@
 
 ITERS = 4
 MESH = pl.DeviceIdType.MESH
+CHUNK = 16
 
 
 def padded_2(block, sides, width):
@@ -109,14 +110,15 @@
     sizes,
     rhs_ref, coef_ref, env_ref,
     sol_ref, out_ref,
-    rhs_own, env_all, coef_all, coef_tab, diag_tab, stack, residual, direction, image, partial, weighted, dots,
+    rhs_own, env_all, coef_all, coef_tab, faces, stack, residual, drive, drive_dir, image_dir, image, keep, down, direction,
     load, rhs_send, rhs_recv, sib_send, sib_recv, env_send, env_recv, envy_send, envy_recv,
-    coef_send, coef_recv, img_send, img_recv, dot_send, dot_recv,
+    coef_send, coef_recv, img_send, img_recv,
 ):
     terms, per, rows, strip, ny, ranks = sizes
     grids, ys = 2, 2
     nx = grids * strip
     half = ys * rows
+    count = terms * per
     gx = lax.axis_index("grid")
     rank = lax.axis_index("rank")
     gz = lax.axis_index("term")
@@ -169,7 +171,7 @@
         return copy
 
     def arrived(block, recv):
-        remote(block, block, dot_send, recv, sibling).wait_recv()
+        remote(block, block, sib_send.at[0], recv, sibling).wait_recv()
 
     def strip_of(x, y):
         return residual.at[pl.ds(x * strip, strip), y, core]
@@ -193,10 +195,12 @@
             block = env_all[o, i].reshape(half, ranks)
             high = block.astype(jnp.bfloat16)
             low = (block - high.astype(jnp.float32)).astype(jnp.bfloat16)
-            at = pl.ds(pl.multiple_of((o * per + i) * half, half), half)
-            stack[at, 0:ranks] = high
-            stack[at, ranks : 2 * ranks] = low
-            stack[at, 2 * ranks : 3 * ranks] = high
+            for c in range(half // CHUNK):
+                at = pl.ds(pl.multiple_of(c * count * CHUNK + (o * per + i) * CHUNK, CHUNK), CHUNK)
+                piece = slice(c * CHUNK, (c + 1) * CHUNK)
+                stack[at, 0:ranks] = high[piece]
+                stack[at, ranks : 2 * ranks] = low[piece]
+                stack[at, 2 * ranks : 3 * ranks] = high[piece]
 
     def cross(i):
         o = origins[i]
@@ -227,102 +231,128 @@
                 k = z * per + i
                 coef_tab[x, k : k + 1, :] = coef_all[z, x // strip, i, x % strip : x % strip + 1, :]
     for x in range(nx):
-        diag_tab[x] = 0.5 * neighbours(lambda j: coef_tab[j], x, nx)
+        here = coef_tab[x]
+        lane = lax.broadcasted_iota(jnp.int32, here.shape, 1)
+        faces[0, x] = 2.0 * here + 0.5 * neighbours(lambda j: coef_tab[j], x, nx)
+        faces[1, x] = jnp.where(lane == ny - 1, 0.0, 0.5 * (here + pltpu.roll(here, ny - 1, 1)))
+        faces[2, x] = jnp.where(lane == 0, 0.0, 0.5 * (here + pltpu.roll(here, 1, 1)))
+        if x > 0:
+            faces[3, x] = 0.5 * (here + coef_tab[x - 1])
+        if x < nx - 1:
+            faces[4, x] = 0.5 * (here + coef_tab[x + 1])
     for copy in sibs:
         copy.wait_recv()
-    square = jnp.zeros((ranks, ny), jnp.float32)
-    for x in range(nx):
-        field = residual[x].reshape(ranks, ny)
-        direction[x] = field
-        square = square + field * field
-    norm_now = total_sum(square)
     for o in [gz] + origins:
         crossed_into_stack(o)
     for copy in sent:
         copy.wait_send()
 
-    count = terms * per
-
-    def product(x):
-        field = direction[x]
-        wide = 2.0 * field - 0.5 * neighbours(lambda j: direction[j], x, nx)
-        plain = jnp.dot(stack[...], split3(field), preferred_element_type=jnp.float32)
-        spread = jnp.dot(stack[...], split3(wide), preferred_element_type=jnp.float32)
-        total = jnp.zeros((half, ny), jnp.float32)
-        inner = jnp.zeros((half, ny), jnp.float32)
-        for k in range(count):
-            c = coef_tab[x, k : k + 1, :]
-            d = diag_tab[x, k : k + 1, :]
-            u = plain[k * half : (k + 1) * half]
-            total = total + c * spread[k * half : (k + 1) * half] + d * u
-            inner = inner + c * u
-        partial[x] = total
-        weighted[x] = inner
-
-    def finish(x, slot):
-        value = partial[x] - 0.5 * neighbours(lambda j: weighted[j], x, nx)
-        image[slot, x, :, core] = value.reshape(ys, rows, ny)
-
     def image_copy(x, slot):
         block = image.at[slot, x, :, core]
         return remote(block, block, img_send.at[slot, x], img_recv.at[slot, x], sibling)
 
-    def operate(slot, send):
-        for x in range(nx + 1):
-            if x < nx:
-                product(x)
+    def emit(slot, x, c, value):
+        per_y = rows // CHUNK
+        image[slot, x, c // per_y, core, (c % per_y) * CHUNK : (c % per_y + 1) * CHUNK, :] = value
+
+    def product(x, field, slot):
+        parts = split3(field)
+        for c in range(half // CHUNK):
+            span = slice(c * count * CHUNK, (c + 1) * count * CHUNK)
+            block = jnp.dot(stack[span, :], parts, preferred_element_type=jnp.float32)
+            sums = [None] * 5
+            for k in range(count):
+                term = block[k * CHUNK : (k + 1) * CHUNK]
+                for a in range(5):
+                    if (a == 3 and x == 0) or (a == 4 and x == nx - 1):
+                        continue
+                    value = faces[a, x, k : k + 1, :] * term
+                    sums[a] = value if sums[a] is None else sums[a] + value
+            value = sums[0] - pltpu.roll(sums[1], 1, 1) - pltpu.roll(sums[2], ny - 1, 1)
+            piece = slice(c * CHUNK, (c + 1) * CHUNK)
             if x > 0:
-                finish(x - 1, slot)
-                if send:
-                    image_copy(x - 1, slot).start()
-
-    strips = pl.ds(gx * strip, strip)
-
-    def iteration(step, norm_now):
-        slot = step % 2
-        operate(slot, True)
-        product_sum = jnp.zeros((ranks, ny), jnp.float32)
+                value = value - down[x - 1, piece, :]
+                emit(slot, x - 1, c, keep[x - 1, piece, :] - sums[3])
+            if x < nx - 1:
+                down[x, piece, :] = sums[4]
+                keep[x, piece, :] = value
+            else:
+                emit(slot, x, c, value)
+        if x > 0:
+            image_copy(x - 1, slot).start()
+        if x == nx - 1:
+            image_copy(x, slot).start()
+
+    mine = pl.ds(pl.multiple_of(rank * rows, rows), rows)
+
+    def folded(v):
+        return jnp.sum(v.reshape(v.shape[0] // 8, 8, v.shape[1]), axis=0)
+
+    square = jnp.zeros((8, ny), jnp.float32)
+    for x in range(nx):
+        field = residual[x].reshape(ranks, ny)
+        square = square + folded(field * field)
+        product(x, field, 0)
+    norm = total_sum(square)
+
+    alpha = beta = None
+    for step in range(ITERS):
+        square = jnp.zeros((8, ny), jnp.float32)
+        cross_sum = jnp.zeros((8, ny), jnp.float32)
+        if step == 1:
+            for i in range(strip):
+                field = residual[gx * strip + i, gy, core]
+                direction[i] = field
+                sol_ref[i] = alpha * field
+        elif step > 1:
+            for i in range(strip):
+                field = residual[gx * strip + i, gy, core] + beta * direction[i]
+                direction[i] = field
+                sol_ref[i] = sol_ref[i] + alpha * field
         for x in range(nx):
-            image_copy(x, slot).wait_recv()
-            product_sum = product_sum + direction[x] * image[slot, x].reshape(ranks, ny)
-        alpha = norm_now / total_sum(product_sum)
-        square = jnp.zeros((ranks, ny), jnp.float32)
-        for x in range(nx):
-            fresh = residual[x].reshape(ranks, ny) - alpha * image[slot, x].reshape(ranks, ny)
-            residual[x] = fresh.reshape(ys, 2, rows, ny)
-            square = square + fresh * fresh
-        norm_next = total_sum(square)
-        beta = norm_next / norm_now
-        mine = pl.ds(pl.multiple_of(rank * rows, rows), rows)
-        for i in range(strip):
-            sol_ref[i] = sol_ref[i] + alpha * direction[gx * strip + i, mine, :]
-        for x in range(nx):
-            direction[x] = residual[x].reshape(ranks, ny) + beta * direction[x]
+            image_copy(x, step).wait_recv()
+            for y in range(ys):
+                for j in range(2):
+                    at = slice((y * 2 + j) * rows, (y * 2 + j + 1) * rows)
+                    fresh = image[step, x, y, j]
+                    left = residual[x, y, j]
+                    if step == 0:
+                        now = fresh
+                    else:
+                        old = drive[x, at, :]
+                        if step == 1:
+                            first, second = old, fresh
+                        else:
+                            first = old + beta * image_dir[x, at, :]
+                            second = fresh + beta * drive_dir[x, at, :]
+                        image_dir[x, at, :] = first
+                        if step < ITERS - 1:
+                            drive_dir[x, at, :] = second
+                        left = left - alpha * first
+                        now = old - alpha * second
+                        residual[x, y, j] = left
+                        square = square + folded(left * left)
+                    drive[x, at, :] = now
+                    cross_sum = cross_sum + folded(left * now)
+            if step < ITERS - 1:
+                product(x, drive[x], step + 1)
+        slope = total_sum(cross_sum)
+        if step == 0:
+            alpha = norm / slope
+        else:
+            fresh_norm = total_sum(square)
+            beta = fresh_norm / norm
+            alpha = fresh_norm / (slope - beta * fresh_norm / alpha)
+            norm = fresh_norm
+
+    for i in range(strip):
+        x = gx * strip + i
+        left = residual[x, gy, core]
+        sol_ref[i] = sol_ref[i] + alpha * (left + beta * direction[i])
+        out_ref[i] = left - alpha * (drive[x, mine, :] + beta * image_dir[x, mine, :])
+    for slot in range(ITERS):
         for x in range(nx):
             image_copy(x, slot).wait_send()
-        return norm_next
-
-    sol_ref[...] = jnp.zeros_like(sol_ref)
-    norm_now = lax.fori_loop(0, ITERS - 1, iteration, norm_now)
-
-    slot = (ITERS - 1) % 2
-    operate(slot, False)
-    mine = pl.ds(pl.multiple_of(rank * rows, rows), rows)
-    part = jnp.zeros((rows, ny), jnp.float32)
-    for x in range(nx):
-        for y in range(ys):
-            field = direction[x, pl.ds(pl.multiple_of((y * 2 + core) * rows, rows), rows), :]
-            part = part + field * image[slot, x, y, core]
-    dots[core] = jnp.broadcast_to(total_sum(part), (8, 128))
-    copy = remote(dots.at[core], dots.at[core], dot_send, dot_recv, sibling)
-    copy.start()
-    copy.wait()
-    both = dots[0] + dots[1]
-    alpha = norm_now / both[0:1, 0:1]
-    for i in range(strip):
-        x = gx * strip + i
-        sol_ref[i] = sol_ref[i] + alpha * direction[x, mine, :]
-        out_ref[i] = residual[x, gy, core] - alpha * image[slot, x, gy, core]
 
 
 def fused(mesh, rhs, coef, env):
@@ -345,22 +375,23 @@
             pltpu.VMEM((terms, per, ys, rows, ranks), f32),
             pltpu.VMEM((terms, grids, per, strip, ny), f32),
             pltpu.VMEM((nx, count, ny), f32),
-            pltpu.VMEM((nx, count, ny), f32),
+            pltpu.VMEM((5, nx, count, ny), f32),
             pltpu.VMEM((count * half, 3 * ranks), jnp.bfloat16),
             pltpu.VMEM((nx, ys, 2, rows, ny), f32),
             pltpu.VMEM((nx, ranks, ny), f32),
-            pltpu.VMEM((2, nx, ys, 2, rows, ny), f32),
+            pltpu.VMEM((nx, ranks, ny), f32),
+            pltpu.VMEM((nx, ranks, ny), f32),
+            pltpu.VMEM((ITERS, nx, ys, 2, rows, ny), f32),
             pltpu.VMEM((nx, half, ny), f32),
             pltpu.VMEM((nx, half, ny), f32),
-            pltpu.VMEM((2, 8, 128), f32),
+            pltpu.VMEM((strip, rows, ny), f32),
             dma((3,)),
             dma((3,)), dma((3,)),
             dma((4,)), dma((4,)),
             dma((terms - 1,)), dma((terms,)),
             dma((terms,)), dma((terms,)),
             dma((terms,)), dma((terms,)),
-            dma((2, nx)), dma((2, nx)),
-            dma, dma,
+            dma((ITERS, nx)), dma((ITERS, nx)),
         ],
         compiler_params=pltpu.CompilerParams(
             collective_id=0, has_side_effects=True, vmem_limit_bytes=63 * 2**20

time: 34 us -> 28.7 us (0.84)
  Pallas kernels: 30.9 us -> 25.6 us
    pallas_call x1, Pallas kernels: 30.9 us -> 25.6 us  [fused(): pl.pallas_call(functools.partial(cg_kernel, sizes), out_shape=(block, blo...]
where the time goes in v1:
time: 28.7 us; the launch traced here: 28.5 us
  Pallas kernels  25.6 us (89%)
  local copies, waits for them, and re-layouts  2.24 us (8%)
  between operations  0.65 us (2%)
    pallas_call x1, Pallas kernels, fused(): pl.pallas_call(functools.partial(cg_kernel, sizes), out_shape=(block, blo...  25.6 us
    unnamed x4, local copies, waits for them, and re-layouts  2.24 us

profile of v1, /device:TPU:0, one launch (start us, length us, event | category | flops | bytes accessed | tf_op | source)
XLA Modules:
  0.0 28.5 jit_solution(4442714628379140614)
XLA Ops:
  0.6 25.6 %shard_map.50 = (f32[2,32,256]{2,1,0:T(8,128)}, f32[2,32,256]{2,1,0:T(8,128)}) custom-call(f32[32,2,256]{2,1,0:T(2,128)} %rhs_ref.1, f32[3,2,256]{2,1,0:T(2,128)} %coef_ref.1, f32[3,32,128]{2,1,0:T(8,128)} %env_ref.1), custom_call_target="tpu_custom_call" | custom-call | tf_op jit(solution)/shard_map/pallas_call | solution.py:368
  26.2 0.0 copy-start
  26.2 1.6 %copy.5 = f32[32,2,256]{2,1,0:T(2,128)} copy(f32[32,2,256]{2,0,1:T(8,128)} %bitcast.3) | data formatting | bytes 131072
  27.8 0.0 copy-done
  27.8 0.7 %copy.6 = f32[32,2,256]{2,1,0:T(2,128)} copy(f32[32,2,256]{2,0,1:T(8,128)S(1)} %bitcast.2) | data formatting | bytes 131072
Async XLA Ops:
  26.2 1.6 %copy-start = (f32[2,32,256]{2,1,0:T(8,128)S(1)}, f32[2,32,256]{2,1,0:T(8,128)}, u32[]{:S(2)}) copy-start(f32[2,32,256]{2,1,0:T(8,128)} %get-tuple-element.5) | copy-start | bytes 196612

commit v2 on v1

--- a/solution.py
+++ b/solution.py
@@ -110,7 +110,7 @@
     sizes,
     rhs_ref, coef_ref, env_ref,
     sol_ref, out_ref,
-    rhs_own, env_all, coef_all, coef_tab, faces, stack, residual, drive, drive_dir, image_dir, image, keep, down, direction,
+    rhs_own, env_all, coef_all, coef_tab, faces, stack, residual, drive, drive_dir, image_dir, image, keep, down, direction, gathered, split_rhs,
     load, rhs_send, rhs_recv, sib_send, sib_recv, env_send, env_recv, envy_send, envy_recv,
     coef_send, coef_recv, img_send, img_recv,
 ):
@@ -181,12 +181,12 @@
 
     own = strip_of(gx, gy)
     for i in (2, 1, 0):
+        push(coef_all.at[gz, gx], coef_send.at[i], coef_recv.at[gz], line[i])
+    for i in (2, 1, 0):
         push(env_line(gz), env_send.at[i], env_recv.at[gz], line[i])
     rhs_y = push(own, rhs_send.at[0], rhs_recv.at[0], over_y)
     rhs_x = push(own, rhs_send.at[1], rhs_recv.at[1], over_x)
     rhs_d = push(own, rhs_send.at[2], rhs_recv.at[2], across)
-    for i in (2, 1, 0):
-        push(coef_all.at[gz, gx], coef_send.at[i], coef_recv.at[gz], line[i])
     push(env_line(gz), envy_send.at[3], envy_recv.at[gz], over_y)
     sibs = [push(own, sib_send.at[0], sib_recv.at[0], sibling)]
 
@@ -215,37 +215,29 @@
         arrived(env_all.at[o, :, 1 - gy], envy_recv.at[o])
         put_stack(o)
 
+    for o in origins:
+        arrived(coef_all.at[o, gx], coef_recv.at[o])
+    coef_x = push(coef_all.at[:, gx], coef_send.at[terms - 1], coef_recv.at[gz], over_x)
     cross(0)
     to_sibling(1, rhs_y, gx, 1 - gy)
     to_sibling(2, rhs_x, 1 - gx, gy)
+    cross(1)
     to_sibling(3, rhs_d, 1 - gx, 1 - gy)
-    cross(1)
-    for o in origins:
-        arrived(coef_all.at[o, gx], coef_recv.at[o])
-    coef_x = push(coef_all.at[:, gx], coef_send.at[terms - 1], coef_recv.at[gz], over_x)
     cross(2)
     coef_x.wait_recv()
     for x in range(nx):
-        for z in range(terms):
-            for i in range(per):
-                k = z * per + i
-                coef_tab[x, k : k + 1, :] = coef_all[z, x // strip, i, x % strip : x % strip + 1, :]
+        for i in range(per):
+            coef_tab[x, :, i, :] = coef_all[:, x // strip, i, x % strip, :]
     for x in range(nx):
         here = coef_tab[x]
-        lane = lax.broadcasted_iota(jnp.int32, here.shape, 1)
+        lane = lax.broadcasted_iota(jnp.int32, here.shape, 2)
         faces[0, x] = 2.0 * here + 0.5 * neighbours(lambda j: coef_tab[j], x, nx)
-        faces[1, x] = jnp.where(lane == ny - 1, 0.0, 0.5 * (here + pltpu.roll(here, ny - 1, 1)))
-        faces[2, x] = jnp.where(lane == 0, 0.0, 0.5 * (here + pltpu.roll(here, 1, 1)))
+        faces[1, x] = jnp.where(lane == ny - 1, 0.0, 0.5 * (here + pltpu.roll(here, ny - 1, 2)))
+        faces[2, x] = jnp.where(lane == 0, 0.0, 0.5 * (here + pltpu.roll(here, 1, 2)))
         if x > 0:
             faces[3, x] = 0.5 * (here + coef_tab[x - 1])
         if x < nx - 1:
             faces[4, x] = 0.5 * (here + coef_tab[x + 1])
-    for copy in sibs:
-        copy.wait_recv()
-    for o in [gz] + origins:
-        crossed_into_stack(o)
-    for copy in sent:
-        copy.wait_send()
 
     def image_copy(x, slot):
         block = image.at[slot, x, :, core]
@@ -254,6 +246,33 @@
     def emit(slot, x, c, value):
         per_y = rows // CHUNK
         image[slot, x, c // per_y, core, (c % per_y) * CHUNK : (c % per_y + 1) * CHUNK, :] = value
+
+    def weighted(block, x, pairs, sums):
+        for n, (z, i) in enumerate(pairs):
+            term = block[n * CHUNK : (n + 1) * CHUNK]
+            for a in range(5):
+                if (a == 3 and x == 0) or (a == 4 and x == nx - 1):
+                    continue
+                value = faces[a, x, z, i : i + 1, :] * term
+                sums[a] = value if sums[a] is None else sums[a] + value
+
+    def settle(x, c, slot, sums):
+        value = sums[0] - pltpu.roll(sums[1], 1, 1) - pltpu.roll(sums[2], ny - 1, 1)
+        piece = slice(c * CHUNK, (c + 1) * CHUNK)
+        if x > 0:
+            value = value - down[x - 1, piece, :]
+            emit(slot, x - 1, c, keep[x - 1, piece, :] - sums[3])
+        if x < nx - 1:
+            down[x, piece, :] = sums[4]
+            keep[x, piece, :] = value
+        else:
+            emit(slot, x, c, value)
+
+    def send_rows(x, slot):
+        if x > 0:
+            image_copy(x - 1, slot).start()
+        if x == nx - 1:
+            image_copy(x, slot).start()
 
     def product(x, field, slot):
         parts = split3(field)
@@ -261,39 +280,54 @@
             span = slice(c * count * CHUNK, (c + 1) * count * CHUNK)
             block = jnp.dot(stack[span, :], parts, preferred_element_type=jnp.float32)
             sums = [None] * 5
-            for k in range(count):
-                term = block[k * CHUNK : (k + 1) * CHUNK]
-                for a in range(5):
-                    if (a == 3 and x == 0) or (a == 4 and x == nx - 1):
-                        continue
-                    value = faces[a, x, k : k + 1, :] * term
-                    sums[a] = value if sums[a] is None else sums[a] + value
-            value = sums[0] - pltpu.roll(sums[1], 1, 1) - pltpu.roll(sums[2], ny - 1, 1)
-            piece = slice(c * CHUNK, (c + 1) * CHUNK)
-            if x > 0:
-                value = value - down[x - 1, piece, :]
-                emit(slot, x - 1, c, keep[x - 1, piece, :] - sums[3])
-            if x < nx - 1:
-                down[x, piece, :] = sums[4]
-                keep[x, piece, :] = value
-            else:
-                emit(slot, x, c, value)
-        if x > 0:
-            image_copy(x - 1, slot).start()
-        if x == nx - 1:
-            image_copy(x, slot).start()
+            weighted(block, x, [(z, i) for z in range(terms) for i in range(per)], sums)
+            settle(x, c, slot, sums)
+        send_rows(x, slot)
+
+    def first_product(o, begin, end):
+        wide = per * CHUNK
+        for x in range(nx):
+            lines = [
+                stack[pl.ds(pl.multiple_of((c * terms + o) * wide, CHUNK), wide), :]
+                for c in range(half // CHUNK)
+            ]
+            block = jnp.dot(jnp.concatenate(lines, axis=0), split_rhs[x], preferred_element_type=jnp.float32)
+            for c in range(half // CHUNK):
+                piece = slice(c * CHUNK, (c + 1) * CHUNK)
+                used = [a for a in range(5) if not ((a == 3 and x == 0) or (a == 4 and x == nx - 1))]
+                sums = [None] * 5
+                if not begin:
+                    for a in used:
+                        sums[a] = gathered[a, x, piece, :]
+                weighted(block[c * wide : (c + 1) * wide], x, [(o, i) for i in range(per)], sums)
+                if end:
+                    settle(x, c, 0, sums)
+                else:
+                    for a in used:
+                        gathered[a, x, piece, :] = sums[a]
+            if end:
+                send_rows(x, 0)
 
     mine = pl.ds(pl.multiple_of(rank * rows, rows), rows)
 
     def folded(v):
         return jnp.sum(v.reshape(v.shape[0] // 8, 8, v.shape[1]), axis=0)
 
+    crossed_into_stack(gz)
+    for copy in sibs:
+        copy.wait_recv()
     square = jnp.zeros((8, ny), jnp.float32)
     for x in range(nx):
         field = residual[x].reshape(ranks, ny)
         square = square + folded(field * field)
-        product(x, field, 0)
+        split_rhs[x] = split3(field)
     norm = total_sum(square)
+    first_product(gz, True, False)
+    for i, o in enumerate(origins):
+        crossed_into_stack(o)
+        first_product(o, False, i == len(origins) - 1)
+    for copy in sent:
+        copy.wait_send()
 
     alpha = beta = None
     for step in range(ITERS):
@@ -374,8 +408,8 @@
             pltpu.VMEM((rows, strip, ny), f32),
             pltpu.VMEM((terms, per, ys, rows, ranks), f32),
             pltpu.VMEM((terms, grids, per, strip, ny), f32),
-            pltpu.VMEM((nx, count, ny), f32),
-            pltpu.VMEM((5, nx, count, ny), f32),
+            pltpu.VMEM((nx, terms, per, ny), f32),
+            pltpu.VMEM((5, nx, terms, per, ny), f32),
             pltpu.VMEM((count * half, 3 * ranks), jnp.bfloat16),
             pltpu.VMEM((nx, ys, 2, rows, ny), f32),
             pltpu.VMEM((nx, ranks, ny), f32),
@@ -385,6 +419,8 @@
             pltpu.VMEM((nx, half, ny), f32),
             pltpu.VMEM((nx, half, ny), f32),
             pltpu.VMEM((strip, rows, ny), f32),
+            pltpu.VMEM((5, nx, half, ny), f32),
+            pltpu.VMEM((nx, 3 * ranks, ny), jnp.bfloat16),
             dma((3,)),
             dma((3,)), dma((3,)),
             dma((4,)), dma((4,)),
@@ -397,7 +433,18 @@
             collective_id=0, has_side_effects=True, vmem_limit_bytes=63 * 2**20
         ),
     )(rhs, coef, env)
-    return sol.transpose(1, 0, 2), res.transpose(1, 0, 2)
+    def place(a_ref, b_ref, c_ref, d_ref):
+        for i in range(strip):
+            c_ref[:, i, :] = a_ref[i]
+            d_ref[:, i, :] = b_ref[i]
+
+    final = jax.ShapeDtypeStruct((rows, strip, ny), f32)
+    return pl.pallas_call(
+        place,
+        out_shape=(final, final),
+        in_specs=[pl.BlockSpec(memory_space=pltpu.VMEM)] * 2,
+        out_specs=(pl.BlockSpec(memory_space=pltpu.VMEM),) * 2,
+    )(sol, res)
 
 
 def fits(mesh, rhs):

time: 28.7 us -> 27.7 us (0.965)
  local copies, waits for them, and re-layouts: 2.24 us -> 0 us
  Pallas kernels: 25.6 us -> 26.8 us
    unnamed x4 -> x0, local copies, waits for them, and re-layouts: 2.24 us -> none
    pallas_call x0 -> x1, Pallas kernels: none -> 1.56 us  [fused(): pl.pallas_call(place, out_shape=(final, final), in_specs=[pl.BlockSpec(me...]
    pallas_call x1, Pallas kernels: 25.6 us -> 25.3 us  [fused(): pl.pallas_call(functools.partial(cg_kernel, sizes), out_shape=(block, blo...]
where the time goes in v2:
time: 27.7 us; the launch traced here: 27.5 us
  Pallas kernels  26.8 us (97%)
  between operations  0.64 us (2%)
    pallas_call x1, Pallas kernels, fused(): pl.pallas_call(functools.partial(cg_kernel, sizes), out_shape=(block, blo...  25.3 us
    pallas_call x1, Pallas kernels, fused(): pl.pallas_call(place, out_shape=(final, final), in_specs=[pl.BlockSpec(me...  1.56 us

profile of v2, /device:TPU:0, one launch (start us, length us, event | category | flops | bytes accessed | tf_op | source)
XLA Modules:
  0.0 27.5 jit_solution(2245322905001411920)
XLA Ops:
  0.6 25.3 %shard_map.50 = (f32[2,32,256]{2,1,0:T(8,128)}, f32[2,32,256]{2,1,0:T(8,128)}) custom-call(f32[32,2,256]{2,1,0:T(2,128)} %rhs_ref.1, f32[3,2,256]{2,1,0:T(2,128)} %coef_ref.1, f32[3,32,128]{2,1,0:T(8,128)} %env_ref.1), custom_call_target="tpu_custom_call" | custom-call | tf_op jit(solution)/shard_map/pallas_call | solution.py:402
  25.9 1.6 %shard_map.51 = (f32[32,2,256]{2,1,0:T(2,128)}, f32[32,2,256]{2,1,0:T(2,128)}) custom-call(f32[2,32,256]{2,1,0:T(8,128)} %get-tuple-element.4.a_ref, f32[2,32,256]{2,1,0:T(8,128)} %get-tuple-element.5.b_ref), custom_call_target="tpu_custom_call" | custom-call | tf_op jit(solution)/shard_map/pallas_call | solution.py:442

commit v3 on v2

--- a/solution.py
+++ b/solution.py
@@ -110,9 +110,9 @@
     sizes,
     rhs_ref, coef_ref, env_ref,
     sol_ref, out_ref,
-    rhs_own, env_all, coef_all, coef_tab, faces, stack, residual, drive, drive_dir, image_dir, image, keep, down, direction, gathered, split_rhs,
+    rhs_own, env_all, coef_all, coef_tab, faces, stack, residual, image, keep, down, gathered, split_rhs, trace, gram,
     load, rhs_send, rhs_recv, sib_send, sib_recv, env_send, env_recv, envy_send, envy_recv,
-    coef_send, coef_recv, img_send, img_recv,
+    coef_send, coef_recv, img_send, img_recv, sum_send, sum_recv,
 ):
     terms, per, rows, strip, ny, ranks = sizes
     grids, ys = 2, 2
@@ -240,12 +240,18 @@
             faces[4, x] = 0.5 * (here + coef_tab[x + 1])
 
     def image_copy(x, slot):
-        block = image.at[slot, x, :, core]
+        block = image.at[slot, pl.ds(x, 2 if x == nx - 2 else 1), :, core]
         return remote(block, block, img_send.at[slot, x], img_recv.at[slot, x], sibling)
 
+    per_y = rows // CHUNK
+
+    def vector(t, x, y, span=slice(None)):
+        ref = residual if t == 0 else image.at[t - 1]
+        return ref[x, y, core, span, :]
+
     def emit(slot, x, c, value):
-        per_y = rows // CHUNK
-        image[slot, x, c // per_y, core, (c % per_y) * CHUNK : (c % per_y + 1) * CHUNK, :] = value
+        span = slice((c % per_y) * CHUNK, (c % per_y + 1) * CHUNK)
+        image[slot, x, c // per_y, core, span, :] = value * inverse - vector(slot, x, c // per_y, span)
 
     def weighted(block, x, pairs, sums):
         for n, (z, i) in enumerate(pairs):
@@ -269,10 +275,10 @@
             emit(slot, x, c, value)
 
     def send_rows(x, slot):
-        if x > 0:
+        if slot < ITERS - 1 and x > 0 and x < nx - 1:
             image_copy(x - 1, slot).start()
-        if x == nx - 1:
-            image_copy(x, slot).start()
+        elif slot < ITERS - 1 and x == nx - 1:
+            image_copy(nx - 2, slot).start()
 
     def product(x, field, slot):
         parts = split3(field)
@@ -308,85 +314,139 @@
             if end:
                 send_rows(x, 0)
 
-    mine = pl.ds(pl.multiple_of(rank * rows, rows), rows)
-
     def folded(v):
         return jnp.sum(v.reshape(v.shape[0] // 8, 8, v.shape[1]), axis=0)
+
+    def paired(block, send):
+        return remote(block, block, sum_send.at[send], sum_recv.at[send], sibling)
+
+    def diagonal():
+        shape = (rows, ranks)
+        row = lax.broadcasted_iota(jnp.int32, shape, 0)
+        column = lax.broadcasted_iota(jnp.int32, shape, 1)
+        on = column == row + rank * rows
+        weight = faces[0, 0]
+        for x in range(1, nx):
+            weight = weight + faces[0, x]
+        weight = jnp.sum(weight, axis=2, keepdims=True)
+        total = jnp.zeros((8, ranks), jnp.float32)
+        for z in range(terms):
+            for i in range(per):
+                entries = jnp.where(on, jnp.abs(env_all[z, i, gy]), 0.0)
+                total = total + weight[z, i : i + 1, :] * folded(entries)
+        return total
+
+    def grams(part, pairs):
+        sums = [None] * len(pairs)
+        needed = sorted({t for pair in pairs for t in pair})
+        for x in range(nx):
+            for y in range(ys):
+                fields = {t: vector(t, x, y) for t in needed}
+                for n, (i, j) in enumerate(pairs):
+                    value = folded(fields[i] * fields[j])
+                    sums[n] = value if sums[n] is None else sums[n] + value
+        for value, pair in zip(sums, pairs):
+            line = jnp.sum(sum(value[:, l : l + 128] for l in range(0, ny, 128)), axis=0, keepdims=True)
+            n = order[part].index(pair)
+            gram[part, core, n : n + 1, :] = line
+
+    def gram_copy(part):
+        return paired(gram.at[part, core], part)
+
+    def gram_sums(part):
+        both = jnp.sum(gram[part, 0] + gram[part, 1], axis=1, keepdims=True)
+        return {pair: both[n : n + 1, :] for n, pair in enumerate(order[part])}
+
+    last = ITERS
+    order = (
+        [(i, j) for j in range(last) for i in range(j + 1)],
+        [(i, last) for i in range(last)],
+    )
 
     crossed_into_stack(gz)
     for copy in sibs:
         copy.wait_recv()
-    square = jnp.zeros((8, ny), jnp.float32)
     for x in range(nx):
-        field = residual[x].reshape(ranks, ny)
-        square = square + folded(field * field)
-        split_rhs[x] = split3(field)
-    norm = total_sum(square)
+        split_rhs[x] = split3(residual[x].reshape(ranks, ny))
+    trace[core] = diagonal()
+    trace_copy = paired(trace.at[core], 2)
+    trace_copy.start()
+    gram[...] = jnp.zeros_like(gram)
+    inverse = None
     first_product(gz, True, False)
     for i, o in enumerate(origins):
         crossed_into_stack(o)
+        if i == len(origins) - 1:
+            trace_copy.wait_recv()
+            size = total_sum(trace[0] + trace[1]) * (1.0 / (half * nx * ny))
+            theta = jnp.where(size > 0.0, size, 1.0)
+            inverse = 1.0 / theta
         first_product(o, False, i == len(origins) - 1)
-    for copy in sent:
+    grams(0, [(0, 0), (0, 1), (1, 1)])
+
+    def mixed(left, right, table):
+        total = None
+        for i, a in enumerate(left):
+            inner = None
+            for j, b in enumerate(right):
+                value = b * table[min(i, j), max(i, j)]
+                inner = value if inner is None else inner + value
+            total = a * inner if total is None else total + a * inner
+        return total
+
+    def applied(d):
+        return [d[0]] + [d[j] + d[j - 1] for j in range(1, len(d))] + [d[-1]]
+
+    def updated(sol, left, d, image_d, alpha):
+        sol = [a + alpha * b for a, b in zip(sol, d)] + [alpha * b for b in d[len(sol) :]]
+        left = [a - alpha * b for a, b in zip(left, image_d)] + [-alpha * image_d[-1]]
+        return sol, left
+
+    for step in range(1, ITERS):
+        for x in range(nx):
+            if x < nx - 1:
+                image_copy(x, step - 1).wait_recv()
+            if step == ITERS - 1 and x == nx - 1:
+                gram_copy(0).wait_recv()
+            product(x, image[step - 1, x].reshape(ranks, ny), step)
+        if step < ITERS - 1:
+            grams(0, [(i, step + 1) for i in range(step + 2)])
+            if step == ITERS - 2:
+                gram_copy(0).start()
+
+    table = gram_sums(0)
+    one = jnp.ones_like(theta)
+    sol, left, d, norm = [], [one], [one], table[0, 0]
+    for step in range(ITERS - 1):
+        image_d = applied(d)
+        alpha = norm / mixed(d, image_d, table)
+        sol, left = updated(sol, left, d, image_d, alpha)
+        fresh = mixed(left, left, table)
+        beta = fresh / norm
+        d = [a + beta * b for a, b in zip(left, d)] + [left[-1]]
+        norm = fresh
+    image_d = applied(d)
+    known = mixed(d, image_d[:-1], table)
+
+    grams(1, order[1])
+    copy = gram_copy(1)
+    copy.start()
+    copy.wait_recv()
+    rest = gram_sums(1)
+    tail = sum(d[i] * rest[i, last] for i in range(last))
+    alpha = norm / (known + image_d[-1] * tail)
+    sol, left = updated(sol, left, d, image_d, alpha)
+    sol = [a * inverse for a in sol]
+    for i in range(strip):
+        fields = [vector(t, gx * strip + i, gy) for t in range(ITERS + 1)]
+        sol_ref[i] = sum(a * v for a, v in zip(sol, fields))
+        out_ref[i] = sum(a * v for a, v in zip(left, fields))
+
+    for slot in range(ITERS - 1):
+        for x in range(nx - 1):
+            image_copy(x, slot).wait_send()
+    for copy in sent + [trace_copy, gram_copy(0), gram_copy(1)]:
         copy.wait_send()
-
-    alpha = beta = None
-    for step in range(ITERS):
-        square = jnp.zeros((8, ny), jnp.float32)
-        cross_sum = jnp.zeros((8, ny), jnp.float32)
-        if step == 1:
-            for i in range(strip):
-                field = residual[gx * strip + i, gy, core]
-                direction[i] = field
-                sol_ref[i] = alpha * field
-        elif step > 1:
-            for i in range(strip):
-                field = residual[gx * strip + i, gy, core] + beta * direction[i]
-                direction[i] = field
-                sol_ref[i] = sol_ref[i] + alpha * field
-        for x in range(nx):
-            image_copy(x, step).wait_recv()
-            for y in range(ys):
-                for j in range(2):
-                    at = slice((y * 2 + j) * rows, (y * 2 + j + 1) * rows)
-                    fresh = image[step, x, y, j]
-                    left = residual[x, y, j]
-                    if step == 0:
-                        now = fresh
-                    else:
-                        old = drive[x, at, :]
-                        if step == 1:
-                            first, second = old, fresh
-                        else:
-                            first = old + beta * image_dir[x, at, :]
-                            second = fresh + beta * drive_dir[x, at, :]
-                        image_dir[x, at, :] = first
-                        if step < ITERS - 1:
-                            drive_dir[x, at, :] = second
-                        left = left - alpha * first
-                        now = old - alpha * second
-                        residual[x, y, j] = left
-                        square = square + folded(left * left)
-                    drive[x, at, :] = now
-                    cross_sum = cross_sum + folded(left * now)
-            if step < ITERS - 1:
-                product(x, drive[x], step + 1)
-        slope = total_sum(cross_sum)
-        if step == 0:
-            alpha = norm / slope
-        else:
-            fresh_norm = total_sum(square)
-            beta = fresh_norm / norm
-            alpha = fresh_norm / (slope - beta * fresh_norm / alpha)
-            norm = fresh_norm
-
-    for i in range(strip):
-        x = gx * strip + i
-        left = residual[x, gy, core]
-        sol_ref[i] = sol_ref[i] + alpha * (left + beta * direction[i])
-        out_ref[i] = left - alpha * (drive[x, mine, :] + beta * image_dir[x, mine, :])
-    for slot in range(ITERS):
-        for x in range(nx):
-            image_copy(x, slot).wait_send()
 
 
 def fused(mesh, rhs, coef, env):
@@ -412,15 +472,13 @@
             pltpu.VMEM((5, nx, terms, per, ny), f32),
             pltpu.VMEM((count * half, 3 * ranks), jnp.bfloat16),
             pltpu.VMEM((nx, ys, 2, rows, ny), f32),
-            pltpu.VMEM((nx, ranks, ny), f32),
-            pltpu.VMEM((nx, ranks, ny), f32),
-            pltpu.VMEM((nx, ranks, ny), f32),
             pltpu.VMEM((ITERS, nx, ys, 2, rows, ny), f32),
             pltpu.VMEM((nx, half, ny), f32),
             pltpu.VMEM((nx, half, ny), f32),
-            pltpu.VMEM((strip, rows, ny), f32),
             pltpu.VMEM((5, nx, half, ny), f32),
             pltpu.VMEM((nx, 3 * ranks, ny), jnp.bfloat16),
+            pltpu.VMEM((2, 8, 128), f32),
+            pltpu.VMEM((2, 2, 16, 128), f32),
             dma((3,)),
             dma((3,)), dma((3,)),
             dma((4,)), dma((4,)),
@@ -428,6 +486,7 @@
             dma((terms,)), dma((terms,)),
             dma((terms,)), dma((terms,)),
             dma((ITERS, nx)), dma((ITERS, nx)),
+            dma((3,)), dma((3,)),
         ],
         compiler_params=pltpu.CompilerParams(
             collective_id=0, has_side_effects=True, vmem_limit_bytes=63 * 2**20

time: 27.7 us -> 27.3 us (0.986)
  Pallas kernels: 26.8 us -> 26.4 us
    pallas_call x1, Pallas kernels: 25.3 us -> 24.9 us  [fused(): pl.pallas_call(functools.partial(cg_kernel, sizes), out_shape=(block, blo...]
where the time goes in v3:
time: 27.3 us; the launch traced here: 27.1 us
  Pallas kernels  26.4 us (97%)
  between operations  0.64 us (2%)
    pallas_call x1, Pallas kernels, fused(): pl.pallas_call(functools.partial(cg_kernel, sizes), out_shape=(block, blo...  24.9 us
    pallas_call x1, Pallas kernels, fused(): pl.pallas_call(place, out_shape=(final, final), in_specs=[pl.BlockSpec(me...  1.56 us

profile of v3, /device:TPU:0, one launch (start us, length us, event | category | flops | bytes accessed | tf_op | source)
XLA Modules:
  0.0 27.1 jit_solution(1920298771485070459)
XLA Ops:
  0.6 24.9 %shard_map.50 = (f32[2,32,256]{2,1,0:T(8,128)}, f32[2,32,256]{2,1,0:T(8,128)}) custom-call(f32[32,2,256]{2,1,0:T(2,128)} %rhs_ref.1, f32[3,2,256]{2,1,0:T(2,128)} %coef_ref.1, f32[3,32,128]{2,1,0:T(8,128)} %env_ref.1), custom_call_target="tpu_custom_call" | custom-call | tf_op jit(solution)/shard_map/pallas_call | solution.py:462
  25.5 1.6 %shard_map.51 = (f32[32,2,256]{2,1,0:T(2,128)}, f32[32,2,256]{2,1,0:T(2,128)}) custom-call(f32[2,32,256]{2,1,0:T(8,128)} %get-tuple-element.4.a_ref, f32[2,32,256]{2,1,0:T(8,128)} %get-tuple-element.5.b_ref), custom_call_target="tpu_custom_call" | custom-call | tf_op jit(solution)/shard_map/pallas_call | solution.py:501

commit v4 on v3

--- a/solution.py
+++ b/solution.py
@@ -133,6 +133,15 @@
     over_x, over_y, across = at(1 - gx, gy, gz), at(gx, 1 - gy, gz), at(1 - gx, 1 - gy, gz)
     line = [at(gx, gy, o) for o in origins]
 
+    barrier = pltpu.get_barrier_semaphore()
+
+    def greet(peer):
+        pl.semaphore_signal(barrier, inc=1, device_id=peer, device_id_type=MESH)
+
+    peers = line[::-1] + [across, over_x, over_y, sibling]
+    for peer in peers:
+        greet(peer)
+
     loads = [
         pltpu.make_async_copy(rhs_ref, rhs_own, load.at[0]),
         pltpu.make_async_copy(env_ref, env_all.at[gz, :, gy], load.at[1]),
@@ -141,15 +150,6 @@
     for copy in loads:
         copy.start()
 
-    barrier = pltpu.get_barrier_semaphore()
-
-    def greet(peer):
-        pl.semaphore_signal(barrier, inc=1, device_id=peer, device_id_type=MESH)
-
-    peers = line + [over_x, over_y, across, sibling]
-    for peer in peers:
-        greet(peer)
-
     loads[0].wait()
     for i in range(strip):
         residual[gx * strip + i, gy, core] = rhs_own[:, i, :]
@@ -184,10 +184,10 @@
         push(coef_all.at[gz, gx], coef_send.at[i], coef_recv.at[gz], line[i])
     for i in (2, 1, 0):
         push(env_line(gz), env_send.at[i], env_recv.at[gz], line[i])
+    push(env_line(gz), envy_send.at[3], envy_recv.at[gz], over_y)
     rhs_y = push(own, rhs_send.at[0], rhs_recv.at[0], over_y)
     rhs_x = push(own, rhs_send.at[1], rhs_recv.at[1], over_x)
     rhs_d = push(own, rhs_send.at[2], rhs_recv.at[2], across)
-    push(env_line(gz), envy_send.at[3], envy_recv.at[gz], over_y)
     sibs = [push(own, sib_send.at[0], sib_recv.at[0], sibling)]
 
     def put_stack(o):
@@ -231,13 +231,12 @@
     for x in range(nx):
         here = coef_tab[x]
         lane = lax.broadcasted_iota(jnp.int32, here.shape, 2)
-        faces[0, x] = 2.0 * here + 0.5 * neighbours(lambda j: coef_tab[j], x, nx)
-        faces[1, x] = jnp.where(lane == ny - 1, 0.0, 0.5 * (here + pltpu.roll(here, ny - 1, 2)))
-        faces[2, x] = jnp.where(lane == 0, 0.0, 0.5 * (here + pltpu.roll(here, 1, 2)))
-        if x > 0:
-            faces[3, x] = 0.5 * (here + coef_tab[x - 1])
-        if x < nx - 1:
-            faces[4, x] = 0.5 * (here + coef_tab[x + 1])
+        after = jnp.where(lane == ny - 1, 0.0, pltpu.roll(here, ny - 1, 2))
+        before = jnp.where(lane == 0, 0.0, pltpu.roll(here, 1, 2))
+        faces[0, x] = 0.5 * (here + after)
+        faces[1, x] = 0.5 * (here + before)
+        faces[2, x] = 0.5 * (here + coef_tab[x - 1] if x > 0 else here)
+        faces[3, x] = 0.5 * (here + coef_tab[x + 1] if x < nx - 1 else here)
 
     def image_copy(x, slot):
         block = image.at[slot, pl.ds(x, 2 if x == nx - 2 else 1), :, core]
@@ -256,20 +255,21 @@
     def weighted(block, x, pairs, sums):
         for n, (z, i) in enumerate(pairs):
             term = block[n * CHUNK : (n + 1) * CHUNK]
-            for a in range(5):
-                if (a == 3 and x == 0) or (a == 4 and x == nx - 1):
-                    continue
+            for a in range(4):
                 value = faces[a, x, z, i : i + 1, :] * term
                 sums[a] = value if sums[a] is None else sums[a] + value
 
     def settle(x, c, slot, sums):
-        value = sums[0] - pltpu.roll(sums[1], 1, 1) - pltpu.roll(sums[2], ny - 1, 1)
+        lane = lax.broadcasted_iota(jnp.int32, sums[0].shape, 1)
+        value = (sums[0] + sums[1]) + (sums[2] + sums[3])
+        value = value - jnp.where(lane == 0, 0.0, pltpu.roll(sums[0], 1, 1))
+        value = value - jnp.where(lane == ny - 1, 0.0, pltpu.roll(sums[1], ny - 1, 1))
         piece = slice(c * CHUNK, (c + 1) * CHUNK)
         if x > 0:
             value = value - down[x - 1, piece, :]
-            emit(slot, x - 1, c, keep[x - 1, piece, :] - sums[3])
+            emit(slot, x - 1, c, keep[x - 1, piece, :] - sums[2])
         if x < nx - 1:
-            down[x, piece, :] = sums[4]
+            down[x, piece, :] = sums[3]
             keep[x, piece, :] = value
         else:
             emit(slot, x, c, value)
@@ -285,7 +285,7 @@
         for c in range(half // CHUNK):
             span = slice(c * count * CHUNK, (c + 1) * count * CHUNK)
             block = jnp.dot(stack[span, :], parts, preferred_element_type=jnp.float32)
-            sums = [None] * 5
+            sums = [None] * 4
             weighted(block, x, [(z, i) for z in range(terms) for i in range(per)], sums)
             settle(x, c, slot, sums)
         send_rows(x, slot)
@@ -300,16 +300,15 @@
             block = jnp.dot(jnp.concatenate(lines, axis=0), split_rhs[x], preferred_element_type=jnp.float32)
             for c in range(half // CHUNK):
                 piece = slice(c * CHUNK, (c + 1) * CHUNK)
-                used = [a for a in range(5) if not ((a == 3 and x == 0) or (a == 4 and x == nx - 1))]
-                sums = [None] * 5
+                sums = [None] * 4
                 if not begin:
-                    for a in used:
+                    for a in range(4):
                         sums[a] = gathered[a, x, piece, :]
                 weighted(block[c * wide : (c + 1) * wide], x, [(o, i) for i in range(per)], sums)
                 if end:
                     settle(x, c, 0, sums)
                 else:
-                    for a in used:
+                    for a in range(4):
                         gathered[a, x, piece, :] = sums[a]
             if end:
                 send_rows(x, 0)
@@ -325,9 +324,7 @@
         row = lax.broadcasted_iota(jnp.int32, shape, 0)
         column = lax.broadcasted_iota(jnp.int32, shape, 1)
         on = column == row + rank * rows
-        weight = faces[0, 0]
-        for x in range(1, nx):
-            weight = weight + faces[0, x]
+        weight = sum(faces[a, x] for a in range(4) for x in range(nx))
         weight = jnp.sum(weight, axis=2, keepdims=True)
         total = jnp.zeros((8, ranks), jnp.float32)
         for z in range(terms):
@@ -469,13 +466,13 @@
             pltpu.VMEM((terms, per, ys, rows, ranks), f32),
             pltpu.VMEM((terms, grids, per, strip, ny), f32),
             pltpu.VMEM((nx, terms, per, ny), f32),
-            pltpu.VMEM((5, nx, terms, per, ny), f32),
+            pltpu.VMEM((4, nx, terms, per, ny), f32),
             pltpu.VMEM((count * half, 3 * ranks), jnp.bfloat16),
             pltpu.VMEM((nx, ys, 2, rows, ny), f32),
             pltpu.VMEM((ITERS, nx, ys, 2, rows, ny), f32),
             pltpu.VMEM((nx, half, ny), f32),
             pltpu.VMEM((nx, half, ny), f32),
-            pltpu.VMEM((5, nx, half, ny), f32),
+            pltpu.VMEM((4, nx, half, ny), f32),
             pltpu.VMEM((nx, 3 * ranks, ny), jnp.bfloat16),
             pltpu.VMEM((2, 8, 128), f32),
             pltpu.VMEM((2, 2, 16, 128), f32),

time: 27.3 us -> 27 us (0.989)
    pallas_call x1, Pallas kernels: 24.9 us -> 24.6 us  [fused(): pl.pallas_call(functools.partial(cg_kernel, sizes), out_shape=(block, blo...]
where the time goes in v4:
time: 27 us; the launch traced here: 26.8 us
  Pallas kernels  26.2 us (97%)
  between operations  0.64 us (2%)
    pallas_call x1, Pallas kernels, fused(): pl.pallas_call(functools.partial(cg_kernel, sizes), out_shape=(block, blo...  24.6 us
    pallas_call x1, Pallas kernels, fused(): pl.pallas_call(place, out_shape=(final, final), in_specs=[pl.BlockSpec(me...  1.56 us

profile of v4, /device:TPU:0, one launch (start us, length us, event | category | flops | bytes accessed | tf_op | source)
XLA Modules:
  0.0 26.8 jit_solution(6418128539818101836)
XLA Ops:
  0.6 24.6 %shard_map.50 = (f32[2,32,256]{2,1,0:T(8,128)}, f32[2,32,256]{2,1,0:T(8,128)}) custom-call(f32[32,2,256]{2,1,0:T(2,128)} %rhs_ref.1, f32[3,2,256]{2,1,0:T(2,128)} %coef_ref.1, f32[3,32,128]{2,1,0:T(8,128)} %env_ref.1), custom_call_target="tpu_custom_call" | custom-call | tf_op jit(solution)/shard_map/pallas_call | solution.py:459
  25.2 1.6 %shard_map.51 = (f32[32,2,256]{2,1,0:T(2,128)}, f32[32,2,256]{2,1,0:T(2,128)}) custom-call(f32[2,32,256]{2,1,0:T(8,128)} %get-tuple-element.4.a_ref, f32[2,32,256]{2,1,0:T(8,128)} %get-tuple-element.5.b_ref), custom_call_target="tpu_custom_call" | custom-call | tf_op jit(solution)/shard_map/pallas_call | solution.py:498

commit v5 on v4

--- a/solution.py
+++ b/solution.py
@@ -180,6 +180,7 @@
         return env_all.at[o, :, gy]
 
     own = strip_of(gx, gy)
+    sibs = [push(own, sib_send.at[0], sib_recv.at[0], sibling)]
     for i in (2, 1, 0):
         push(coef_all.at[gz, gx], coef_send.at[i], coef_recv.at[gz], line[i])
     for i in (2, 1, 0):
@@ -188,7 +189,6 @@
     rhs_y = push(own, rhs_send.at[0], rhs_recv.at[0], over_y)
     rhs_x = push(own, rhs_send.at[1], rhs_recv.at[1], over_x)
     rhs_d = push(own, rhs_send.at[2], rhs_recv.at[2], across)
-    sibs = [push(own, sib_send.at[0], sib_recv.at[0], sibling)]
 
     def put_stack(o):
         for i in range(per):
@@ -380,6 +380,8 @@
             inverse = 1.0 / theta
         first_product(o, False, i == len(origins) - 1)
     grams(0, [(0, 0), (0, 1), (1, 1)])
+    for copy in sent + [trace_copy]:
+        copy.wait_send()
 
     def mixed(left, right, table):
         total = None
@@ -410,7 +412,12 @@
             grams(0, [(i, step + 1) for i in range(step + 2)])
             if step == ITERS - 2:
                 gram_copy(0).start()
-
+            for x in range(nx - 1):
+                image_copy(x, step - 1).wait_send()
+
+    grams(1, order[1])
+    copy = gram_copy(1)
+    copy.start()
     table = gram_sums(0)
     one = jnp.ones_like(theta)
     sol, left, d, norm = [], [one], [one], table[0, 0]
@@ -424,26 +431,20 @@
         norm = fresh
     image_d = applied(d)
     known = mixed(d, image_d[:-1], table)
-
-    grams(1, order[1])
-    copy = gram_copy(1)
-    copy.start()
-    copy.wait_recv()
+    mine = []
+    for i in range(strip):
+        fields = [vector(t, gx * strip + i, gy) for t in range(ITERS + 1)]
+        mine.append([sum(a * v for a, v in zip(line, fields)) for line in (sol, d, left, image_d)])
+    for x in range(nx - 1):
+        image_copy(x, ITERS - 2).wait_send()
+    gram_copy(0).wait_send()
+    copy.wait()
     rest = gram_sums(1)
     tail = sum(d[i] * rest[i, last] for i in range(last))
     alpha = norm / (known + image_d[-1] * tail)
-    sol, left = updated(sol, left, d, image_d, alpha)
-    sol = [a * inverse for a in sol]
-    for i in range(strip):
-        fields = [vector(t, gx * strip + i, gy) for t in range(ITERS + 1)]
-        sol_ref[i] = sum(a * v for a, v in zip(sol, fields))
-        out_ref[i] = sum(a * v for a, v in zip(left, fields))
-
-    for slot in range(ITERS - 1):
-        for x in range(nx - 1):
-            image_copy(x, slot).wait_send()
-    for copy in sent + [trace_copy, gram_copy(0), gram_copy(1)]:
-        copy.wait_send()
+    for i, (found, way, rest_left, image_way) in enumerate(mine):
+        sol_ref[i] = (found + alpha * way) * inverse
+        out_ref[i] = rest_left - alpha * image_way
 
 
 def fused(mesh, rhs, coef, env):

time: 27 us -> 26.9 us (level)
  no operation moved by 1% of the time
where the time goes in v5:
time: 26.9 us; the launch traced here: 26.7 us
  Pallas kernels  26.1 us (97%)
  between operations  0.64 us (2%)
    pallas_call x1, Pallas kernels, fused(): pl.pallas_call(functools.partial(cg_kernel, sizes), out_shape=(block, blo...  24.5 us
    pallas_call x1, Pallas kernels, fused(): pl.pallas_call(place, out_shape=(final, final), in_specs=[pl.BlockSpec(me...  1.56 us

profile of v5, /device:TPU:0, one launch (start us, length us, event | category | flops | bytes accessed | tf_op | source)
XLA Modules:
  0.0 26.7 jit_solution(3840473109519349711)
XLA Ops:
  0.6 24.5 %shard_map.50 = (f32[2,32,256]{2,1,0:T(8,128)}, f32[2,32,256]{2,1,0:T(8,128)}) custom-call(f32[32,2,256]{2,1,0:T(2,128)} %rhs_ref.1, f32[3,2,256]{2,1,0:T(2,128)} %coef_ref.1, f32[3,32,128]{2,1,0:T(8,128)} %env_ref.1), custom_call_target="tpu_custom_call" | custom-call | tf_op jit(solution)/shard_map/pallas_call | solution.py:460
  25.1 1.6 %shard_map.51 = (f32[32,2,256]{2,1,0:T(2,128)}, f32[32,2,256]{2,1,0:T(2,128)}) custom-call(f32[2,32,256]{2,1,0:T(8,128)} %get-tuple-element.4.a_ref, f32[2,32,256]{2,1,0:T(8,128)} %get-tuple-element.5.b_ref), custom_call_target="tpu_custom_call" | custom-call | tf_op jit(solution)/shard_map/pallas_call | solution.py:499
